TPU v7x, 128 devices: a whole 4x4x4 slice. The times are simulated.
128 devices in a mesh: dp: 8 (over z, core), shard: 16 (over x, y).
Axes of the slice: x: 4, y: 4, z: 4, core: 2. Of those that a mesh axis runs over, the one named last changes fastest.
Arguments:
- attention_grad: float32 [8, 3968, 3968], P('dp', 'shard'), may hold values from -127 to 127
- attention_error: float32 [8, 3968, 3968], P('dp', 'shard'), may hold values from -64 to 64
- attention_warm: float32 [32, 3968], replicated, may hold values from -6 to 6
- feedforward_grad: float32 [8, 7936, 2048], P('dp', 'shard'), may hold values from -127 to 127
- feedforward_error: float32 [8, 7936, 2048], P('dp', 'shard'), may hold values from -64 to 64
- feedforward_warm: float32 [32, 2048], replicated, may hold values from -6 to 6
Outputs:
- attention_carry: float32 [8, 3968, 3968], P('dp', 'shard')
- feedforward_carry: float32 [8, 7936, 2048], P('dp', 'shard')
- attention_basis: float32 [32, 3968], replicated
- feedforward_basis: float32 [32, 2048], replicated
All inputs are finite; a program needn't handle non-finite values.
Results may differ from a plain program's by a relative error of at most 0.00025.
Values sent between devices are 32-bit elements; how exact they have to be, the bound alone decides.
A program may use at most 128 MiB of HBM per device.

v0:
```python
import functools

import jax
import jax.numpy as jnp
from jax import lax
from jax.experimental import pallas as pl
from jax.experimental.pallas import tpu as pltpu
from jax.sharding import PartitionSpec as P

f32, bf16 = jnp.float32, jnp.bfloat16
MESH = pl.DeviceIdType.MESH
NT = (((1,), (1,)), ((), ()))
NN = (((1,), (0,)), ((), ()))
TN = (((0,), (0,)), ((), ()))
HIGHEST = lax.Precision.HIGHEST

R = 32
HALF = 16
REPLICAS = 8
CHIPS = 64
PLANE = 16
LANES = 128
A_ROWS, A_PAD, A_COLS = 248, 256, 3968
F_ROWS, F_PAD, F_COLS = 496, 512, 2048
ROWS = A_PAD + F_PAD
A_UNITS, F_UNITS = A_COLS // LANES, F_COLS // LANES
UNITS = A_UNITS + F_UNITS
A_STEP, F_STEP = 512, 256
A_FULL, A_TAIL = A_COLS // A_STEP, A_COLS % A_STEP
F_FULL = F_COLS // F_STEP
GROUPS = ((0, 16), (16, 15), (31, 8), (39, 8))


def dot(a, b, dims):
    return lax.dot_general(a, b, dims, preferred_element_type=f32)


def exact(a, b, dims):
    return lax.dot_general(a, b, dims, precision=HIGHEST, preferred_element_type=f32)


def split(x):
    hi = x.astype(bf16)
    return hi, (x - hi.astype(f32)).astype(bf16)


def stacked(x):
    return jnp.concatenate(split(x), axis=0)


def folded(x):
    return x[:R] + x[R:]


def inverse_factors(a):
    lane = lax.broadcasted_iota(jnp.int32, (R, LANES), 1)
    row_of = lax.broadcasted_iota(jnp.int32, (R, LANES), 0)
    for k in range(R):
        row = jnp.broadcast_to(a[k : k + 1, :], (R, LANES))
        first = jnp.broadcast_to(a[:, k : k + 1], (R, LANES))
        second = jnp.broadcast_to(a[:, 64 + k : 65 + k], (R, LANES))
        column = jnp.where(lane < 64, first, second)
        pivot = jnp.broadcast_to(column[k : k + 1, :], (R, LANES))
        factor = jnp.where(row_of > k, column * (1.0 / pivot), 0.0)
        a = a - factor * row
        a = jnp.where(row_of == k, row * lax.rsqrt(pivot), a)
    return a[:, R : 2 * R], a[:, 3 * R :]


def sweeps(
    ag, ae, fg, fe, aw, fw,
    ma, mf, bt, qa, qf,
    sga, sea, sgf, sef, swa, swf, load_sem,
    acc, pbuf, pmate, pz, pfull,
    gs, zl, zp, zs, rr, zg,
    p_send, p_recv, g_send, g_recv, m_send, m_recv,
    rs_send, rs_recv, ag_send, ag_recv, fw_send, fw_recv,
):
    dp, s = lax.axis_index("dp"), lax.axis_index("shard")
    z, c = dp // 2, dp % 2
    j = s * 4 + z
    mate = (z * 2 + (1 - c), s)

    def chip(o):
        return ((o % 4) * 2 + c, o // 4)

    def a_load(col, w, k):
        at = pl.ds(col, w)
        return (
            pltpu.make_async_copy(ag.at[0, :, at], sga.at[:, at], load_sem.at[0, k]),
            pltpu.make_async_copy(ae.at[0, :, at], sea.at[:, at], load_sem.at[1, k]),
        )

    def f_load(col, w, k):
        at = pl.ds(col, w)
        return (
            pltpu.make_async_copy(fg.at[0, :, at], sgf.at[:, at], load_sem.at[0, k]),
            pltpu.make_async_copy(fe.at[0, :, at], sef.at[:, at], load_sem.at[1, k]),
        )

    load_aw = pltpu.make_async_copy(aw, swa, load_sem.at[0, 16])
    load_fw = pltpu.make_async_copy(fw, swf, load_sem.at[1, 16])
    load_aw.start()
    for k in range(A_FULL + 1):
        for copy in a_load(k * A_STEP, A_STEP if k < A_FULL else A_TAIL, k):
            copy.start()
    load_fw.start()
    for k in range(F_FULL):
        for copy in f_load(k * F_STEP, F_STEP, A_FULL + 1 + k):
            copy.start()

    barrier = pltpu.get_barrier_semaphore()

    def greet(k, _):
        pl.semaphore_signal(barrier, 1, device_id=chip((j + k) % CHIPS), device_id_type=MESH)
        return 0

    lax.fori_loop(1, CHIPS, greet, 0)
    pl.semaphore_signal(barrier, 1, device_id=mate, device_id_type=MESH)

    acc[...] = jnp.zeros_like(acc)

    def absorb(copies, sg, se, sw, m, col, w, rows, pad, base):
        for copy in copies:
            copy.wait()
        at = pl.ds(col, w)
        value = jnp.concatenate([sg[:, at] + se[:, at], jnp.zeros((pad - rows, w), f32)], axis=0)
        hi, lo = split(value)
        m[0, :, at] = hi
        m[1, :, at] = lo
        x = stacked(sw[:, at])
        acc[:, base : base + pad] += dot(x, hi, NT) + dot(x, lo, NT)

    def a_absorb(k, _):
        col = pl.multiple_of(k * A_STEP, A_STEP)
        absorb(a_load(col, A_STEP, k), sga, sea, swa, ma, col, A_STEP, A_ROWS, A_PAD, 0)
        return 0

    def f_absorb(k, _):
        col = pl.multiple_of(k * F_STEP, F_STEP)
        absorb(f_load(col, F_STEP, A_FULL + 1 + k), sgf, sef, swf, mf, col, F_STEP, F_ROWS, F_PAD, A_PAD)
        return 0

    load_aw.wait()
    lax.fori_loop(0, A_FULL, a_absorb, 0)
    absorb(a_load(A_FULL * A_STEP, A_TAIL, A_FULL), sga, sea, swa, ma, A_FULL * A_STEP, A_TAIL, A_ROWS, A_PAD, 0)
    load_fw.wait()
    lax.fori_loop(0, F_FULL, f_absorb, 0)
    pl.semaphore_wait(barrier, CHIPS)

    def units_of(it, first, count):
        def unit(u):
            return jnp.concatenate([zg[it, 0, u], zg[it, 1, u]], axis=0)

        return jnp.concatenate([unit(first + i) for i in range(count)], axis=1)

    def left_again():
        acc[...] = jnp.zeros_like(acc)

        def a_piece(first, col, w):
            x = stacked(units_of(0, first, w // LANES))
            at = pl.ds(col, w)
            acc[:, :A_PAD] += dot(x, ma[0, :, at], NT) + dot(x, ma[1, :, at], NT)

        def a_step(k, _):
            a_piece(k * (A_STEP // LANES), pl.multiple_of(k * A_STEP, A_STEP), A_STEP)
            return 0

        def f_step(k, _):
            x = stacked(units_of(0, A_UNITS + k * (F_STEP // LANES), F_STEP // LANES))
            at = pl.ds(pl.multiple_of(k * F_STEP, F_STEP), F_STEP)
            acc[:, A_PAD:] += dot(x, mf[0, :, at], NT) + dot(x, mf[1, :, at], NT)
            return 0

        lax.fori_loop(0, A_FULL, a_step, 0)
        a_piece(A_FULL * (A_STEP // LANES), A_FULL * A_STEP, A_TAIL)
        lax.fori_loop(0, F_FULL, f_step, 0)

    def remote(src, dst, send, recv, to):
        return pltpu.make_async_remote_copy(src, dst, send, recv, device_id=to, device_id_type=MESH)

    inverses = None
    left = None
    for it in range(2):
        if it == 1:
            left_again()

        pbuf[it] = folded(acc[...])
        mine, other = pl.ds(pl.multiple_of(c * HALF, HALF), HALF), pl.ds(pl.multiple_of((1 - c) * HALF, HALF), HALF)
        copy = remote(pbuf.at[it, other], pmate.at[it], p_send.at[it, 0], p_recv.at[it, 0], mate)
        copy.start()
        copy.wait()
        pz[it, z] = pbuf[it, mine] + pmate[it]
        copies = []
        for i in (2, 1, 3):
            to = (z + i) % 4
            copy = remote(pz.at[it, z], pz.at[it, z], p_send.at[it, i], p_recv.at[it, 1 + z], (to * 2 + c, s))
            copy.start()
            copies.append(copy)
        for i in (1, 3, 2):
            o = (z + i) % 4
            remote(pz.at[it, o], pz.at[it, o], p_send.at[it, i], p_recv.at[it, 1 + o], mate).wait_recv()
        pfull[it, mine] = (pz[it, 0] + pz[it, 1]) + (pz[it, 2] + pz[it, 3])
        copy = remote(pfull.at[it, mine], pfull.at[it, mine], p_send.at[it, 4], p_recv.at[it, 5], mate)
        copy.start()
        for sent in copies:
            sent.wait_send()
        copy.wait_send()
        remote(pfull.at[it, other], pfull.at[it, other], p_send.at[it, 4], p_recv.at[it, 5], mate).wait_recv()
        left = pfull[it]
        if it == 1:
            left = jnp.concatenate(
                [exact(inverses[0], left[:, :A_PAD], NN), exact(inverses[1], left[:, A_PAD:], NN)], axis=1
            ) * (1.0 / REPLICAS)

        la, lf = left[:, :A_PAD], left[:, A_PAD:]
        ga, gf = exact(la, la, NT), exact(lf, lf, NT)
        gs[it, s] = jnp.concatenate([ga[:HALF], ga[HALF:], gf[:HALF], gf[HALF:]], axis=1)

        def send_gram(k, _, it=it):
            to = (s + k) % PLANE
            remote(gs.at[it, s], gs.at[it, s], g_send.at[it, to], g_recv.at[it, s], (dp, to)).start()
            return 0

        lax.fori_loop(1, PLANE, send_gram, 0)

        pa, pf = stacked(la), stacked(lf)

        def a_right(col, first, w, it=it, pa=pa):
            at = pl.ds(col, w)
            y = folded(dot(pa, ma[0, :, at], NN)) + folded(dot(pa, ma[1, :, at], NN))
            for i in range(w // LANES):
                zl[it, 0, first + i] = y[:HALF, i * LANES : (i + 1) * LANES]
                zl[it, 1, first + i] = y[HALF:, i * LANES : (i + 1) * LANES]

        def a_right_step(k, _):
            a_right(pl.multiple_of(k * A_STEP, A_STEP), k * (A_STEP // LANES), A_STEP)
            return 0

        def f_right_step(k, _, it=it, pf=pf):
            at = pl.ds(pl.multiple_of(k * F_STEP, F_STEP), F_STEP)
            first = A_UNITS + k * (F_STEP // LANES)
            y = folded(dot(pf, mf[0, :, at], NN)) + folded(dot(pf, mf[1, :, at], NN))
            for i in range(F_STEP // LANES):
                zl[it, 0, first + i] = y[:HALF, i * LANES : (i + 1) * LANES]
                zl[it, 1, first + i] = y[HALF:, i * LANES : (i + 1) * LANES]
            return 0

        def to_mate(g, it=it):
            at = pl.ds(*GROUPS[g])
            return remote(zl.at[it, 1 - c, at], zp.at[it, at], m_send.at[it, g], m_recv.at[it, g], mate)

        lax.fori_loop(0, 4, a_right_step, 0)
        to_mate(0).start()
        lax.fori_loop(4, A_FULL, a_right_step, 0)
        a_right(A_FULL * A_STEP, A_FULL * (A_STEP // LANES), A_TAIL)
        to_mate(1).start()
        lax.fori_loop(0, 4, f_right_step, 0)
        to_mate(2).start()
        lax.fori_loop(4, F_FULL, f_right_step, 0)
        to_mate(3).start()
        for g, (first, count) in enumerate(GROUPS):
            to_mate(g).wait()
            at = pl.ds(first, count)
            zs[it, at] = zl[it, c, at] + zp[it, at]

        def scatter(k, _, it=it):
            o = (j + k) % CHIPS

            @pl.when(o < UNITS)
            def _():
                remote(zs.at[it, o], rr.at[it, j], rs_send.at[it, o], rs_recv.at[it, j], chip(o)).start()

            return 0

        lax.fori_loop(1, CHIPS, scatter, 0)

        def gram_done(k, _, it=it):
            o = (s + k) % PLANE
            remote(gs.at[it, s], gs.at[it, o], g_send.at[it, o], g_recv.at[it, o], mate).wait()
            return 0

        lax.fori_loop(1, PLANE, gram_done, 0)
        gram = gs[it, 0]
        for o in range(1, PLANE):
            gram = gram + gs[it, o]
        eye = (
            lax.broadcasted_iota(jnp.int32, (R, R), 0) == lax.broadcasted_iota(jnp.int32, (R, R), 1)
        ).astype(f32)
        ga = jnp.concatenate([gram[:, :R], gram[:, R : 2 * R]], axis=0)
        gf = jnp.concatenate([gram[:, 2 * R : 3 * R], gram[:, 3 * R :]], axis=0)
        inverses = inverse_factors(jnp.concatenate([ga, eye, gf, eye], axis=1))
        if it == 1:
            bt[...] = jnp.concatenate([exact(inverses[0], la, NN), exact(inverses[1], lf, NN)], axis=1)

        def scattered(o, _, it=it):
            @pl.when(o != j)
            def _():
                remote(zs.at[it, o], rr.at[it, o], rs_send.at[it, o], rs_recv.at[it, o], mate).wait_send()

            return 0

        lax.fori_loop(0, UNITS, scattered, 0)

        @pl.when(j < UNITS)
        def _(it=it):
            rr[it, j] = zs[it, j]

            def arrived(k, _):
                o = (j + k) % CHIPS
                remote(rr.at[it, o], rr.at[it, o], rs_send.at[it, 0], rs_recv.at[it, o], mate).wait_recv()
                return 0

            lax.fori_loop(1, CHIPS, arrived, 0)
            zg[it, c, j] = jnp.sum(rr[it], axis=0)

            def gather(k, _):
                o = (j + k) % CHIPS
                remote(zg.at[it, c, j], zg.at[it, c, j], ag_send.at[it, o], ag_recv.at[it, j], chip(o)).start()
                return 0

            lax.fori_loop(1, CHIPS, gather, 0)

            def gathered(k, _):
                o = (j + k) % CHIPS
                remote(zg.at[it, c, j], zg.at[it, c, j], ag_send.at[it, o], ag_recv.at[it, j], mate).wait_send()
                return 0

            lax.fori_loop(1, CHIPS, gathered, 0)

        for g, (first, count) in enumerate(GROUPS):

            def landed(o, _, it=it):
                @pl.when(o != j)
                def _():
                    remote(zg.at[it, c, o], zg.at[it, c, o], ag_send.at[it, 0], ag_recv.at[it, o], mate).wait_recv()

                return 0

            lax.fori_loop(first, first + count, landed, 0)
            at = pl.ds(first, count)
            remote(zg.at[it, c, at], zg.at[it, c, at], fw_send.at[it, g], fw_recv.at[it, g], mate).start()
        for g, (first, count) in enumerate(GROUPS):
            at = pl.ds(first, count)
            remote(zg.at[it, 1 - c, at], zg.at[it, 1 - c, at], fw_send.at[it, g], fw_recv.at[it, g], mate).wait()

    def normal(inverse, x):
        hi, lo = split(x)
        return dot(inverse, jnp.concatenate([hi, lo, hi, lo], axis=0), NN) * (1.0 / REPLICAS)

    def wide(inverse):
        hi, lo = split(inverse)
        return jnp.concatenate([hi, hi, lo, lo], axis=1)

    wa, wf = wide(inverses[0]), wide(inverses[1])

    def a_out(k, _):
        qa[:, pl.ds(pl.multiple_of(k * A_STEP, A_STEP), A_STEP)] = normal(wa, units_of(1, k * 4, 4))
        return 0

    def f_out(k, _):
        qf[:, pl.ds(pl.multiple_of(k * 512, 512), 512)] = normal(wf, units_of(1, A_UNITS + k * 4, 4))
        return 0

    lax.fori_loop(0, A_FULL, a_out, 0)
    qa[:, A_FULL * A_STEP :] = normal(wa, units_of(1, A_FULL * 4, 3))
    lax.fori_loop(0, 4, f_out, 0)


def carries(ma, mf, bt, qa, qf, ca, cf, oa, of, sa, sf, sem, q_sem):
    copies = [pltpu.make_async_copy(qa, oa, q_sem.at[0]), pltpu.make_async_copy(qf, of, q_sem.at[1])]
    for copy in copies:
        copy.start()
    bh, bl = split(bt[...])
    basis = jnp.concatenate([bh, bh, bl, bl], axis=0)
    n = 0
    for m, q, out, stage, rows, base, pad, cols, step in (
        (ma, qa, ca, sa, A_ROWS, 0, A_PAD, A_COLS, 512),
        (mf, qf, cf, sf, F_ROWS, A_PAD, F_PAD, F_COLS, 256),
    ):
        for col in range(0, cols, step):
            at = slice(col, min(col + step, cols))
            qh, ql = split(q[:, at])
            low = dot(basis[:, base : base + pad], jnp.concatenate([qh, ql, qh, ql], axis=0), TN)
            full = m[0, :, at].astype(f32) + m[1, :, at].astype(f32) - low
            stage[:, at] = full[:rows]
            copy = pltpu.make_async_copy(stage.at[:, at], out.at[0, :, at], sem.at[n])
            copy.start()
            copies.append(copy)
            n += 1
    for copy in copies:
        copy.wait()


def shards(ag, ae, aw, fg, fe, fw):
    hbm = pl.BlockSpec(memory_space=pl.ANY)
    vmem = pl.BlockSpec(memory_space=pltpu.VMEM)
    dma = pltpu.SemaphoreType.DMA
    ma, mf, bt, qa, qf = pl.pallas_call(
        sweeps,
        name="sweeps",
        out_shape=(
            pltpu.VMEM((2, A_PAD, A_COLS), bf16),
            pltpu.VMEM((2, F_PAD, F_COLS), bf16),
            pltpu.VMEM((R, ROWS), f32),
            pltpu.VMEM((R, A_COLS), f32),
            pltpu.VMEM((R, F_COLS), f32),
        ),
        in_specs=[hbm] * 6,
        out_specs=[vmem] * 5,
        scratch_shapes=[
            pltpu.VMEM((A_ROWS, A_COLS), f32),
            pltpu.VMEM((A_ROWS, A_COLS), f32),
            pltpu.VMEM((F_ROWS, F_COLS), f32),
            pltpu.VMEM((F_ROWS, F_COLS), f32),
            pltpu.VMEM((R, A_COLS), f32),
            pltpu.VMEM((R, F_COLS), f32),
            dma((2, 17)),
            pltpu.VMEM((2 * R, ROWS), f32),
            pltpu.VMEM((2, R, ROWS), f32),
            pltpu.VMEM((2, HALF, ROWS), f32),
            pltpu.VMEM((2, 4, HALF, ROWS), f32),
            pltpu.VMEM((2, R, ROWS), f32),
            pltpu.VMEM((2, PLANE, HALF, LANES), f32),
            pltpu.VMEM((2, 2, UNITS, HALF, LANES), f32),
            pltpu.VMEM((2, UNITS, HALF, LANES), f32),
            pltpu.VMEM((2, UNITS, HALF, LANES), f32),
            pltpu.VMEM((2, CHIPS, HALF, LANES), f32),
            pltpu.VMEM((2, 2, UNITS, HALF, LANES), f32),
            dma((2, 5)),
            dma((2, 6)),
            dma((2, PLANE)),
            dma((2, PLANE)),
            dma((2, 4)),
            dma((2, 4)),
            dma((2, CHIPS)),
            dma((2, CHIPS)),
            dma((2, CHIPS)),
            dma((2, CHIPS)),
            dma((2, 4)),
            dma((2, 4)),
        ],
        compiler_params=pltpu.CompilerParams(
            collective_id=0, has_side_effects=True, vmem_limit_bytes=46 * 2**20
        ),
    )(ag, ae, fg, fe, aw, fw)
    return tuple(
        pl.pallas_call(
            carries,
            name="carries",
            out_shape=(
                jax.ShapeDtypeStruct((1, A_ROWS, A_COLS), f32),
                jax.ShapeDtypeStruct((1, F_ROWS, F_COLS), f32),
                jax.ShapeDtypeStruct((R, A_COLS), f32),
                jax.ShapeDtypeStruct((R, F_COLS), f32),
            ),
            in_specs=[vmem] * 5,
            out_specs=[hbm] * 4,
            scratch_shapes=[
                pltpu.VMEM((A_ROWS, A_COLS), f32),
                pltpu.VMEM((F_ROWS, F_COLS), f32),
                dma((16,)),
                dma((2,)),
            ],
            compiler_params=pltpu.CompilerParams(vmem_limit_bytes=24 * 2**20),
        )(ma, mf, bt, qa, qf)
    )


def solution(mesh):
    rows = P("dp", "shard", None)
    return jax.shard_map(
        shards,
        mesh=mesh,
        in_specs=(rows, rows, P(), rows, rows, P()),
        out_specs=(rows, rows, P(), P()),
        check_vma=False,
    )
```

profile of v0, /device:TPU:1, one launch (start us, length us, event | category | flops | bytes accessed | tf_op | source)
XLA Modules:
  0.0 95.9 jit_solution(2415000432411197891)
XLA Ops:
  0.6 91.4 %sweeps.1 = (bf16[2,256,3968]{2,1,0:T(8,128)(2,1)S(1)}, bf16[2,512,2048]{2,1,0:T(8,128)(2,1)S(1)}, f32[32,768]{1,0:T(8,128)S(1)}, f32[32,3968]{1,0:T(8,128)S(1)}, f32[32,2048]{1,0:T(8,128)S(1)}) custom-call(f32[1,248,3968]{2,1,0:T(8,128)} %ag.1, f32[1,248,3968]{2,1,0:T(8,128)} %ae.1, f32[1,496,2048]{2,1,0:T(8,128)} %fg.1, f32[1,496,2048]{2,1,0:T(8,128)} %fe.1, ...), custom_call_target="tpu_custom_call" | custom-call | tf_op jit(solution)/shard_map/sweeps/pallas_call | solution.py:399
  92.1 3.8 %carries.1 = (f32[1,248,3968]{2,1,0:T(8,128)}, f32[1,496,2048]{2,1,0:T(8,128)}, f32[32,3968]{1,0:T(8,128)}, f32[32,2048]{1,0:T(8,128)}) custom-call(bf16[2,256,3968]{2,1,0:T(8,128)(2,1)S(1)} %get-tuple-element.9.ma, bf16[2,512,2048]{2,1,0:T(8,128)(2,1)S(1)} %get-tuple-element.10.mf, f32[32,768]{1,0:T(8,128)S(1)} %get-tuple-element.11.bt, ...), custom_call_target="tpu_custom_call" | custom-call | tf_op jit(solution)/shard_map/carries/pallas_call | solution.py:448
where the time goes:
time: 96 us; the launch traced here: 95.9 us
  Pallas kernels  95.3 us (99%)
    pallas_call x1, Pallas kernels, shards(): pl.pallas_call(sweeps, name='sweeps', out_shape=(pltpu.VMEM((2, A_PAD, A_...  91.4 us
    pallas_call x1, Pallas kernels, shards(): pl.pallas_call(carries, name='carries', out_shape=(jax.ShapeDtypeStruct((...  3.84 us

commit v1 on v0

v1 whole, which is shorter than its diff:
```python
import functools

import jax
import jax.numpy as jnp
from jax import lax
from jax.experimental import pallas as pl
from jax.experimental.pallas import tpu as pltpu
from jax.sharding import PartitionSpec as P

f32, bf16 = jnp.float32, jnp.bfloat16
MESH = pl.DeviceIdType.MESH
NT = (((1,), (1,)), ((), ()))
NN = (((1,), (0,)), ((), ()))
TN = (((0,), (0,)), ((), ()))
HIGHEST = lax.Precision.HIGHEST

R = 32
HALF = 16
REPLICAS = 8
CHIPS = 64
PLANE = 16
LANES = 128
A_ROWS, A_PAD, A_COLS = 248, 256, 3968
F_ROWS, F_PAD, F_COLS = 496, 512, 2048
ROWS = A_PAD + F_PAD
A_UNITS, F_UNITS = A_COLS // LANES, F_COLS // LANES
F_FIRST, UNITS = 32, 48
A_STEP, F_STEP = 512, 256
A_FULL, A_TAIL = A_COLS // A_STEP, A_COLS % A_STEP
F_FULL = F_COLS // F_STEP
GROUPS = ((0, 16), (16, 15), (32, 16))


def dot(a, b, dims):
    return lax.dot_general(a, b, dims, preferred_element_type=f32)


def exact(a, b, dims):
    return lax.dot_general(a, b, dims, precision=HIGHEST, preferred_element_type=f32)


def split(x):
    hi = x.astype(bf16)
    return hi, (x - hi.astype(f32)).astype(bf16)


def stacked(x):
    return jnp.concatenate(split(x), axis=0)


def folded(x):
    return x[:R] + x[R:]


def inverse_factors(a):
    lane = lax.broadcasted_iota(jnp.int32, (R, LANES), 1)
    row_of = lax.broadcasted_iota(jnp.int32, (R, LANES), 0)
    for k in range(R):
        row = jnp.broadcast_to(a[k : k + 1, :], (R, LANES))
        first = jnp.broadcast_to(a[:, k : k + 1], (R, LANES))
        second = jnp.broadcast_to(a[:, 64 + k : 65 + k], (R, LANES))
        column = jnp.where(lane < 64, first, second)
        pivot = jnp.broadcast_to(column[k : k + 1, :], (R, LANES))
        factor = jnp.where(row_of > k, column * (1.0 / pivot), 0.0)
        a = a - factor * row
        a = jnp.where(row_of == k, row * lax.rsqrt(pivot), a)
    return a[:, R : 2 * R], a[:, 3 * R :]


def sweeps(
    ag, ae, fg, fe, aw, fw,
    ma, mf, bt, qa, qf,
    sa, sf, swa, swf, load_sem, warm_sem,
    acc, a_part, f_part, a_mate, f_mate, a_z, f_z, a_sum, f_sum,
    gs, zl, zp, zs, rr, zg,
    p_send, p_recv, g_send, g_recv, m_send, m_recv,
    rs_send, rs_recv, ag_send, ag_recv, fw_send, fw_recv,
):
    dp, s = lax.axis_index("dp"), lax.axis_index("shard")
    z, c = lax.div(dp, 2), lax.rem(dp, 2)
    x, y = lax.div(s, 4), lax.rem(s, 4)
    j = s * 4 + z
    mate = (z * 2 + (1 - c), s)
    unit = lax.rem(27 * j, CHIPS)
    owner = jnp.logical_and(unit < UNITS, unit != A_UNITS)

    along = [lax.rem(z + i, 4) * 2 + c for i in range(4)]

    def each_peer(act):
        def column(k, _):
            to = lax.rem(x + 2 + lax.div(k, 4), 4) * 4 + lax.rem(y + 2 + lax.rem(k, 4), 4)
            for i in (2, 1, 3):
                act((along[i], to))

            @pl.when(to != s)
            def _():
                act((dp, to))

            return 0

        lax.fori_loop(0, PLANE, column, 0)

    def remote(src, dst, send, recv, to):
        return pltpu.make_async_remote_copy(src, dst, send, recv, device_id=to, device_id_type=MESH)

    def loads(grad, error, stage, col, w, k):
        at = pl.ds(col, w)
        return (
            pltpu.make_async_copy(grad.at[0, :, at], stage.at[0, :, at], load_sem.at[k]),
            pltpu.make_async_copy(error.at[0, :, at], stage.at[1, :, at], load_sem.at[k]),
        )

    load_aw = pltpu.make_async_copy(aw, swa, warm_sem.at[0])
    load_fw = pltpu.make_async_copy(fw, swf, warm_sem.at[1])
    load_aw.start()
    for k in range(A_FULL + 1):
        for copy in loads(ag, ae, sa, k * A_STEP, A_STEP if k < A_FULL else A_TAIL, k):
            copy.start()
    load_fw.start()
    for k in range(F_FULL):
        for copy in loads(fg, fe, sf, k * F_STEP, F_STEP, A_FULL + 1 + k):
            copy.start()

    barrier = pltpu.get_barrier_semaphore()

    def greet(to):
        pl.semaphore_signal(barrier, 1, device_id=to, device_id_type=MESH)

    each_peer(greet)
    pl.semaphore_signal(barrier, 1, device_id=mate, device_id_type=MESH)
    acc[...] = jnp.zeros_like(acc)

    def absorb(stage, sw, m, col, w, rows, pad, base, k):
        at = pl.ds(col, w)
        pltpu.make_async_copy(stage.at[:, :, at], stage.at[:, :, at], load_sem.at[k]).wait()
        value = jnp.concatenate([stage[0, :, at] + stage[1, :, at], jnp.zeros((pad - rows, w), f32)], axis=0)
        hi, lo = split(value)
        m[0, :, at] = hi
        m[1, :, at] = lo
        terms = stacked(sw[:, at])
        acc[:, base : base + pad] += dot(terms, hi, NT) + dot(terms, lo, NT)

    def a_absorb(k, _):
        absorb(sa, swa, ma, pl.multiple_of(k * A_STEP, A_STEP), A_STEP, A_ROWS, A_PAD, 0, k)
        return 0

    def f_absorb(k, _):
        col = pl.multiple_of(k * F_STEP, F_STEP)
        absorb(sf, swf, mf, col, F_STEP, F_ROWS, F_PAD, A_PAD, A_FULL + 1 + k)
        return 0

    def joined(it, first, count):
        return jnp.concatenate(
            [jnp.concatenate([zg[it, 0, first + i], zg[it, 1, first + i]], axis=0) for i in range(count)], axis=1
        )

    def a_left(first, col, w):
        terms = stacked(joined(0, first, w // LANES))
        at = pl.ds(col, w)
        acc[:, :A_PAD] += dot(terms, ma[0, :, at], NT) + dot(terms, ma[1, :, at], NT)

    def a_left_step(k, _):
        a_left(k * (A_STEP // LANES), pl.multiple_of(k * A_STEP, A_STEP), A_STEP)
        return 0

    def f_left_step(k, _):
        terms = stacked(joined(0, F_FIRST + k * (F_STEP // LANES), F_STEP // LANES))
        at = pl.ds(pl.multiple_of(k * F_STEP, F_STEP), F_STEP)
        acc[:, A_PAD:] += dot(terms, mf[0, :, at], NT) + dot(terms, mf[1, :, at], NT)
        return 0

    mine = pl.ds(pl.multiple_of(c * HALF, HALF), HALF)
    other = pl.ds(pl.multiple_of((1 - c) * HALF, HALF), HALF)
    rows_of = (slice(0, A_PAD), slice(A_PAD, ROWS))
    part, from_mate, along_z, whole = (a_part, f_part), (a_mate, f_mate), (a_z, f_z), (a_sum, f_sum)

    def halves(it, m):
        return remote(part[m].at[it, other], from_mate[m].at[it], p_send.at[it, m, 0], p_recv.at[it, m, 0], mate)

    def start_halves(it, m):
        part[m][it] = folded(acc[:, rows_of[m]])
        halves(it, m).start()

    def start_z(it, m):
        halves(it, m).wait()
        along_z[m][it, z] = part[m][it, mine] + from_mate[m][it]
        for i in (2, 1, 3):
            at = along_z[m].at[it, z]
            remote(at, at, p_send.at[it, m, 1], p_recv.at[it, m, 1], (along[i], s)).start()

    def start_back(it, m):
        three = along_z[m].at[it, pl.ds(0, 3)]
        remote(three, three, p_send.at[it, m, 1], p_recv.at[it, m, 1], mate).wait()
        terms = along_z[m]
        whole[m][it, mine] = (terms[it, 0] + terms[it, 1]) + (terms[it, 2] + terms[it, 3])
        at = whole[m].at[it, mine]
        remote(at, at, p_send.at[it, m, 2], p_recv.at[it, m, 2], mate).start()

    def finish_left(it, m, inverses):
        at = whole[m].at[it, other]
        remote(at, at, p_send.at[it, m, 2], p_recv.at[it, m, 2], mate).wait()
        left = whole[m][it]
        if it == 1:
            left = exact(inverses[m], left, NN) * (1.0 / REPLICAS)
        return left

    def keep(it, first, product):
        for i in range(product.shape[1] // LANES):
            zl[it, 0, first + i] = product[:HALF, i * LANES : (i + 1) * LANES]
            zl[it, 1, first + i] = product[HALF:, i * LANES : (i + 1) * LANES]

    def right(it, m, terms, first, col, w):
        matrix = (ma, mf)[m]
        at = pl.ds(col, w)
        keep(it, first, folded(dot(terms, matrix[0, :, at], NN)) + folded(dot(terms, matrix[1, :, at], NN)))

    def right_steps(it, m, terms, begin, end):
        def step(k, _):
            first = k * (A_STEP // LANES) + (0, F_FIRST)[m]
            right(it, m, terms, first, pl.multiple_of(k * A_STEP, A_STEP), A_STEP)
            return 0

        lax.fori_loop(begin, end, step, 0)

    def to_mate(it, g):
        at = pl.ds(*GROUPS[g])
        return remote(zl.at[it, 1 - c, at], zp.at[it, at], m_send.at[it, g], m_recv.at[it, g], mate)

    def scatter(it, g):
        first, count = GROUPS[g]
        to_mate(it, g).wait()
        at = pl.ds(first, count)
        zs[it, at] = zl[it, c, at] + zp[it, at]

        def send(k, _):
            u = first + lax.rem(j + k, count)
            o = lax.rem(19 * u, CHIPS)

            @pl.when(o != j)
            def _():
                to = (lax.rem(o, 4) * 2 + c, lax.div(o, 4))
                remote(zs.at[it, u], rr.at[it, j], rs_send.at[it], rs_recv.at[it], to).start()

            return 0

        lax.fori_loop(0, count, send, 0)

    eye = (lax.broadcasted_iota(jnp.int32, (R, R), 0) == lax.broadcasted_iota(jnp.int32, (R, R), 1)).astype(f32)

    def start_gram(it, la, lf):
        ga, gf = exact(la, la, NT), exact(lf, lf, NT)
        gs[it, s] = jnp.concatenate([ga[:HALF], ga[HALF:], gf[:HALF], gf[HALF:]], axis=1)

        def send(k, _):
            at = gs.at[it, s]
            remote(at, at, g_send.at[it], g_recv.at[it], (dp, lax.rem(s + k, PLANE))).start()
            return 0

        lax.fori_loop(1, PLANE, send, 0)

    def finish_gram(it):
        others = gs.at[it, pl.ds(0, PLANE - 1)]
        remote(others, others, g_send.at[it], g_recv.at[it], mate).wait()
        gram = gs[it, 0]
        for o in range(1, PLANE):
            gram = gram + gs[it, o]
        ga = jnp.concatenate([gram[:, :R], gram[:, R : 2 * R]], axis=0)
        gf = jnp.concatenate([gram[:, 2 * R : 3 * R], gram[:, 3 * R :]], axis=0)
        return inverse_factors(jnp.concatenate([ga, eye, gf, eye], axis=1))

    def gather(it):
        @pl.when(owner)
        def _():
            rr[it, j] = zs[it, unit]
            others = rr.at[it, pl.ds(0, CHIPS - 1)]
            remote(others, others, rs_send.at[it], rs_recv.at[it], mate).wait_recv()
            zg[it, c, unit] = jnp.sum(rr[it], axis=0)

            group = lax.div(unit, 16)

            def send(to):
                at = zg.at[it, c, unit]
                remote(at, at, ag_send.at[it], ag_recv.at[it, group], to).start()

            each_peer(send)

    def sent(it):
        @pl.when(owner)
        def _():
            some = zs.at[it, pl.ds(0, 46)]
            remote(some, some, rs_send.at[it], rs_recv.at[it], mate).wait_send()
            others = rr.at[it, pl.ds(0, CHIPS - 1)]
            remote(others, others, ag_send.at[it], rs_recv.at[it], mate).wait_send()

        @pl.when(jnp.logical_not(owner))
        def _():
            some = zs.at[it, pl.ds(0, 47)]
            remote(some, some, rs_send.at[it], rs_recv.at[it], mate).wait_send()

    def handed(it, g):
        first, count = GROUPS[g]
        at = zg.at[it, c, pl.ds(first, count)]
        return remote(at, at, fw_send.at[it, g], fw_recv.at[it, g], mate)

    def hand_on(it, g):
        first, count = GROUPS[g]
        own = jnp.logical_and(unit >= first, unit < first + count)

        @pl.when(own)
        def _():
            some = zg.at[it, c, pl.ds(first, count - 1)]
            remote(some, some, ag_send.at[it], ag_recv.at[it, g], mate).wait_recv()

        @pl.when(jnp.logical_not(own))
        def _():
            some = zg.at[it, c, pl.ds(first, count)]
            remote(some, some, ag_send.at[it], ag_recv.at[it, g], mate).wait_recv()

        handed(it, g).start()

    def normal(inverse, value):
        hi, lo = split(value)
        return dot(inverse, jnp.concatenate([hi, lo, hi, lo], axis=0), NN) * (1.0 / REPLICAS)

    def wide(inverse):
        hi, lo = split(inverse)
        return jnp.concatenate([hi, hi, lo, lo], axis=1)

    def a_out(inverse, begin, end):
        def step(k, _):
            qa[:, pl.ds(pl.multiple_of(k * A_STEP, A_STEP), A_STEP)] = normal(inverse, joined(1, k * 4, 4))
            return 0

        lax.fori_loop(begin, end, step, 0)

    def f_out(inverse):
        def step(k, _):
            qf[:, pl.ds(pl.multiple_of(k * A_STEP, A_STEP), A_STEP)] = normal(inverse, joined(1, F_FIRST + k * 4, 4))
            return 0

        lax.fori_loop(0, F_COLS // A_STEP, step, 0)

    inverses = None
    for it in range(2):
        if it == 0:
            load_aw.wait()
            lax.fori_loop(0, A_FULL, a_absorb, 0)
            absorb(sa, swa, ma, A_FULL * A_STEP, A_TAIL, A_ROWS, A_PAD, 0, A_FULL)
            pl.semaphore_wait(barrier, CHIPS)
            start_halves(it, 0)
            load_fw.wait()
            lax.fori_loop(0, 4, f_absorb, 0)
            start_z(it, 0)
            lax.fori_loop(4, F_FULL, f_absorb, 0)
        else:
            acc[...] = jnp.zeros_like(acc)
            hand_on(0, 0)
            hand_on(0, 1)
            handed(0, 0).wait()
            lax.fori_loop(0, 4, a_left_step, 0)
            hand_on(0, 2)
            handed(0, 1).wait()
            lax.fori_loop(4, A_FULL, a_left_step, 0)
            a_left(A_FULL * (A_STEP // LANES), A_FULL * A_STEP, A_TAIL)
            start_halves(it, 0)
            handed(0, 2).wait()
            lax.fori_loop(0, 4, f_left_step, 0)
            start_z(it, 0)
            lax.fori_loop(4, F_FULL, f_left_step, 0)
        start_halves(it, 1)
        if it == 0:
            start_back(it, 0)
            start_z(it, 1)
        else:
            start_z(it, 1)
            start_back(it, 0)
        la = finish_left(it, 0, inverses)
        terms = stacked(la)
        right_steps(it, 0, terms, 0, 4)
        to_mate(it, 0).start()
        right_steps(it, 0, terms, 4, A_FULL)
        right(it, 0, terms, A_FULL * (A_STEP // LANES), A_FULL * A_STEP, A_TAIL)
        to_mate(it, 1).start()
        if it == 0:
            scatter(it, 0)
            start_back(it, 1)
        else:
            start_back(it, 1)
            scatter(it, 0)
        lf = finish_left(it, 1, inverses)
        terms = stacked(lf)
        right_steps(it, 1, terms, 0, F_COLS // A_STEP)
        to_mate(it, 2).start()
        scatter(it, 1)
        scatter(it, 2)
        start_gram(it, la, lf)
        gather(it)
        inverses = finish_gram(it)
        if it == 1:
            bt[...] = jnp.concatenate([exact(inverses[0], la, NN), exact(inverses[1], lf, NN)], axis=1)
        sent(it)

    wa, wf = wide(inverses[0]), wide(inverses[1])
    hand_on(1, 0)
    hand_on(1, 1)
    handed(1, 0).wait()
    a_out(wa, 0, 4)
    hand_on(1, 2)
    handed(1, 1).wait()
    a_out(wa, 4, A_FULL)
    qa[:, A_FULL * A_STEP :] = normal(wa, joined(1, A_FULL * 4, A_TAIL // LANES))
    handed(1, 2).wait()
    f_out(wf)


def carries(ma, mf, bt, qa, qf, ca, cf, oa, of, sa, sf, sem, q_sem):
    copies = [pltpu.make_async_copy(qa, oa, q_sem.at[0]), pltpu.make_async_copy(qf, of, q_sem.at[1])]
    for copy in copies:
        copy.start()
    bh, bl = split(bt[...])
    basis = jnp.concatenate([bh, bh, bl, bl], axis=0)
    n = 0
    for m, q, out, stage, rows, base, pad, cols, step in (
        (ma, qa, ca, sa, A_ROWS, 0, A_PAD, A_COLS, 512),
        (mf, qf, cf, sf, F_ROWS, A_PAD, F_PAD, F_COLS, 256),
    ):
        for col in range(0, cols, step):
            at = slice(col, min(col + step, cols))
            qh, ql = split(q[:, at])
            low = dot(basis[:, base : base + pad], jnp.concatenate([qh, ql, qh, ql], axis=0), TN)
            full = m[0, :, at].astype(f32) + m[1, :, at].astype(f32) - low
            stage[:, at] = full[:rows]
            copy = pltpu.make_async_copy(stage.at[:, at], out.at[0, :, at], sem.at[n])
            copy.start()
            copies.append(copy)
            n += 1
    for copy in copies:
        copy.wait()


def kernel_one(ag, ae, aw, fg, fe, fw):
    hbm = pl.BlockSpec(memory_space=pl.ANY)
    vmem = pl.BlockSpec(memory_space=pltpu.VMEM)
    dma = pltpu.SemaphoreType.DMA
    return pl.pallas_call(
        sweeps,
        name="sweeps",
        out_shape=(
            pltpu.VMEM((2, A_PAD, A_COLS), bf16),
            pltpu.VMEM((2, F_PAD, F_COLS), bf16),
            pltpu.VMEM((R, ROWS), f32),
            pltpu.VMEM((R, A_COLS), f32),
            pltpu.VMEM((R, F_COLS), f32),
        ),
        in_specs=[hbm] * 6,
        out_specs=[vmem] * 5,
        scratch_shapes=[
            pltpu.VMEM((2, A_ROWS, A_COLS), f32),
            pltpu.VMEM((2, F_ROWS, F_COLS), f32),
            pltpu.VMEM((R, A_COLS), f32),
            pltpu.VMEM((R, F_COLS), f32),
            dma((A_FULL + 1 + F_FULL,)),
            dma((2,)),
            pltpu.VMEM((2 * R, ROWS), f32),
            pltpu.VMEM((2, R, A_PAD), f32),
            pltpu.VMEM((2, R, F_PAD), f32),
            pltpu.VMEM((2, HALF, A_PAD), f32),
            pltpu.VMEM((2, HALF, F_PAD), f32),
            pltpu.VMEM((2, 4, HALF, A_PAD), f32),
            pltpu.VMEM((2, 4, HALF, F_PAD), f32),
            pltpu.VMEM((2, R, A_PAD), f32),
            pltpu.VMEM((2, R, F_PAD), f32),
            pltpu.VMEM((2, PLANE, HALF, LANES), f32),
            pltpu.VMEM((2, 2, UNITS, HALF, LANES), f32),
            pltpu.VMEM((2, UNITS, HALF, LANES), f32),
            pltpu.VMEM((2, UNITS, HALF, LANES), f32),
            pltpu.VMEM((2, CHIPS, HALF, LANES), f32),
            pltpu.VMEM((2, 2, UNITS, HALF, LANES), f32),
            dma((2, 2, 3)),
            dma((2, 2, 3)),
            dma((2,)),
            dma((2,)),
            dma((2, 3)),
            dma((2, 3)),
            dma((2,)),
            dma((2,)),
            dma((2,)),
            dma((2, 3)),
            dma((2, 3)),
            dma((2, 3)),
        ],
        compiler_params=pltpu.CompilerParams(
            collective_id=0, has_side_effects=True, vmem_limit_bytes=46 * 2**20
        ),
    )(ag, ae, fg, fe, aw, fw)


def shards(*args):
    hbm = pl.BlockSpec(memory_space=pl.ANY)
    vmem = pl.BlockSpec(memory_space=pltpu.VMEM)
    dma = pltpu.SemaphoreType.DMA
    return tuple(
        pl.pallas_call(
            carries,
            name="carries",
            out_shape=(
                jax.ShapeDtypeStruct((1, A_ROWS, A_COLS), f32),
                jax.ShapeDtypeStruct((1, F_ROWS, F_COLS), f32),
                jax.ShapeDtypeStruct((R, A_COLS), f32),
                jax.ShapeDtypeStruct((R, F_COLS), f32),
            ),
            in_specs=[vmem] * 5,
            out_specs=[hbm] * 4,
            scratch_shapes=[
                pltpu.VMEM((A_ROWS, A_COLS), f32),
                pltpu.VMEM((F_ROWS, F_COLS), f32),
                dma((16,)),
                dma((2,)),
            ],
            compiler_params=pltpu.CompilerParams(vmem_limit_bytes=24 * 2**20),
        )(*kernel_one(*args))
    )


def solution(mesh):
    rows = P("dp", "shard", None)
    return jax.shard_map(
        shards,
        mesh=mesh,
        in_specs=(rows, rows, P(), rows, rows, P()),
        out_specs=(rows, rows, P(), P()),
        check_vma=False,
    )
```

time: 96 us -> 79.6 us (0.83)
  Pallas kernels: 95.3 us -> 78.8 us
    pallas_call x1, Pallas kernels: 91.4 us -> 75 us  [kernel_one(): pl.pallas_call(sweeps, name='sweeps', out_shape=(pltpu.VMEM((2, A_PAD, A_...]
where the time goes in v1:
time: 79.6 us; the launch traced here: 79.5 us
  Pallas kernels  78.8 us (99%)
    pallas_call x1, Pallas kernels, kernel_one(): pl.pallas_call(sweeps, name='sweeps', out_shape=(pltpu.VMEM((2, A_PAD, A_...  75 us
    pallas_call x1, Pallas kernels, shards(): pl.pallas_call(carries, name='carries', out_shape=(jax.ShapeDtypeStruct((...  3.84 us

profile of v1, /device:TPU:1, one launch (start us, length us, event | category | flops | bytes accessed | tf_op | source)
XLA Modules:
  0.0 79.5 jit_solution(864725150072387630)
XLA Ops:
  0.6 75.0 %sweeps.1 = (bf16[2,256,3968]{2,1,0:T(8,128)(2,1)S(1)}, bf16[2,512,2048]{2,1,0:T(8,128)(2,1)S(1)}, f32[32,768]{1,0:T(8,128)S(1)}, f32[32,3968]{1,0:T(8,128)S(1)}, f32[32,2048]{1,0:T(8,128)S(1)}) custom-call(f32[1,248,3968]{2,1,0:T(8,128)} %ag.1, f32[1,248,3968]{2,1,0:T(8,128)} %ae.1, f32[1,496,2048]{2,1,0:T(8,128)} %fg.1, f32[1,496,2048]{2,1,0:T(8,128)} %fe.1, ...), custom_call_target="tpu_custom_call" | custom-call | tf_op jit(solution)/shard_map/sweeps/pallas_call | solution.py:445
  75.6 3.8 %carries.1 = (f32[1,248,3968]{2,1,0:T(8,128)}, f32[1,496,2048]{2,1,0:T(8,128)}, f32[32,3968]{1,0:T(8,128)}, f32[32,2048]{1,0:T(8,128)}) custom-call(bf16[2,256,3968]{2,1,0:T(8,128)(2,1)S(1)} %get-tuple-element.9.ma, bf16[2,512,2048]{2,1,0:T(8,128)(2,1)S(1)} %get-tuple-element.10.mf, f32[32,768]{1,0:T(8,128)S(1)} %get-tuple-element.11.bt, ...), custom_call_target="tpu_custom_call" | custom-call | tf_op jit(solution)/shard_map/carries/pallas_call | solution.py:503

commit v2 on v1

--- a/solution.py
+++ b/solution.py
@@ -12,7 +12,6 @@
 NT = (((1,), (1,)), ((), ()))
 NN = (((1,), (0,)), ((), ()))
 TN = (((0,), (0,)), ((), ()))
-HIGHEST = lax.Precision.HIGHEST
 
 R = 32
 HALF = 16
@@ -23,20 +22,19 @@
 A_ROWS, A_PAD, A_COLS = 248, 256, 3968
 F_ROWS, F_PAD, F_COLS = 496, 512, 2048
 ROWS = A_PAD + F_PAD
+A_HALF, F_HALF = A_PAD // 2, F_PAD // 2
 A_UNITS, F_UNITS = A_COLS // LANES, F_COLS // LANES
 F_FIRST, UNITS = 32, 48
-A_STEP, F_STEP = 512, 256
+A_STEP, F_STEP = 512, 512
+A_LOAD, F_LOAD = 1024, 512
 A_FULL, A_TAIL = A_COLS // A_STEP, A_COLS % A_STEP
-F_FULL = F_COLS // F_STEP
+A_LOADS, A_REST = A_COLS // A_LOAD, A_COLS % A_LOAD
+F_LOADS = F_COLS // F_LOAD
 GROUPS = ((0, 16), (16, 15), (32, 16))
 
 
 def dot(a, b, dims):
     return lax.dot_general(a, b, dims, preferred_element_type=f32)
-
-
-def exact(a, b, dims):
-    return lax.dot_general(a, b, dims, precision=HIGHEST, preferred_element_type=f32)
 
 
 def split(x):
@@ -44,12 +42,37 @@
     return hi, (x - hi.astype(f32)).astype(bf16)
 
 
+def split3(x):
+    hi = x.astype(bf16)
+    rest = x - hi.astype(f32)
+    mid = rest.astype(bf16)
+    return hi, mid, (rest - mid.astype(f32)).astype(bf16)
+
+
+def applied(inverse, x):
+    a, b, c = split3(inverse)
+    h, m, l = split3(x)
+    return dot(jnp.concatenate([a, a, a, b, b, c], axis=1), jnp.concatenate([h, m, l, h, m, h], axis=0), NN)
+
+
+def gram_of(x):
+    terms = jnp.concatenate(split3(x), axis=0)
+    g = dot(terms, terms, NT)
+    g = g[:R] + g[R : 2 * R] + g[2 * R :]
+    return g[:, :R] + g[:, R : 2 * R] + g[:, 2 * R :]
+
+
 def stacked(x):
     return jnp.concatenate(split(x), axis=0)
 
 
 def folded(x):
     return x[:R] + x[R:]
+
+
+def twice(x):
+    terms = stacked(x)
+    return jnp.concatenate([terms, terms], axis=1)
 
 
 def inverse_factors(a):
@@ -71,9 +94,10 @@
     ag, ae, fg, fe, aw, fw,
     ma, mf, bt, qa, qf,
     sa, sf, swa, swf, load_sem, warm_sem,
-    acc, a_part, f_part, a_mate, f_mate, a_z, f_z, a_sum, f_sum,
-    gs, zl, zp, zs, rr, zg,
-    p_send, p_recv, g_send, g_recv, m_send, m_recv,
+    ra, rf, ta, tf, t_send, t_recv,
+    acc, a_z, f_z, b_part,
+    gs, gt, gm, gz, zl, zp, zs, rr, zg,
+    p_send, p_recv, b_send, b_recv, g_send, g_recv, h_send, h_recv, m_send, m_recv,
     rs_send, rs_recv, ag_send, ag_recv, fw_send, fw_recv,
 ):
     dp, s = lax.axis_index("dp"), lax.axis_index("shard")
@@ -113,12 +137,12 @@
     load_aw = pltpu.make_async_copy(aw, swa, warm_sem.at[0])
     load_fw = pltpu.make_async_copy(fw, swf, warm_sem.at[1])
     load_aw.start()
-    for k in range(A_FULL + 1):
-        for copy in loads(ag, ae, sa, k * A_STEP, A_STEP if k < A_FULL else A_TAIL, k):
+    for k in range(A_LOADS + 1):
+        for copy in loads(ag, ae, sa, k * A_LOAD, A_LOAD if k < A_LOADS else A_REST, k):
             copy.start()
     load_fw.start()
-    for k in range(F_FULL):
-        for copy in loads(fg, fe, sf, k * F_STEP, F_STEP, A_FULL + 1 + k):
+    for k in range(F_LOADS):
+        for copy in loads(fg, fe, sf, k * F_LOAD, F_LOAD, A_LOADS + 1 + k):
             copy.start()
 
     barrier = pltpu.get_barrier_semaphore()
@@ -130,24 +154,33 @@
     pl.semaphore_signal(barrier, 1, device_id=mate, device_id_type=MESH)
     acc[...] = jnp.zeros_like(acc)
 
-    def absorb(stage, sw, m, col, w, rows, pad, base, k):
+    lanes_of = (slice(0, A_PAD), slice(A_PAD, ROWS))
+
+    ma[A_ROWS:] = jnp.zeros((A_PAD - A_ROWS, A_COLS), f32)
+    mf[F_ROWS:] = jnp.zeros((F_PAD - F_ROWS, F_COLS), f32)
+
+    def rows_kept(core, m):
+        half = (A_HALF, F_HALF)[m]
+        return pl.ds(pl.multiple_of(core * half, half), half)
+
+    def half_rows(m, col, w, k):
+        at = pl.ds(col, w)
+        source = (ma, mf)[m].at[rows_kept(1 - c, m), at]
+        return remote(source, (ra, rf)[m].at[:, at], t_send.at[k], t_recv.at[k], mate)
+
+    def absorb(stage, m, rows, col, w, k):
         at = pl.ds(col, w)
         pltpu.make_async_copy(stage.at[:, :, at], stage.at[:, :, at], load_sem.at[k]).wait()
-        value = jnp.concatenate([stage[0, :, at] + stage[1, :, at], jnp.zeros((pad - rows, w), f32)], axis=0)
-        hi, lo = split(value)
-        m[0, :, at] = hi
-        m[1, :, at] = lo
-        terms = stacked(sw[:, at])
-        acc[:, base : base + pad] += dot(terms, hi, NT) + dot(terms, lo, NT)
-
-    def a_absorb(k, _):
-        absorb(sa, swa, ma, pl.multiple_of(k * A_STEP, A_STEP), A_STEP, A_ROWS, A_PAD, 0, k)
-        return 0
-
-    def f_absorb(k, _):
-        col = pl.multiple_of(k * F_STEP, F_STEP)
-        absorb(sf, swf, mf, col, F_STEP, F_ROWS, F_PAD, A_PAD, A_FULL + 1 + k)
-        return 0
+        (ma, mf)[m][:rows, at] = stage[0, :, at] + stage[1, :, at]
+        half_rows(m, col, w, k).start()
+
+    def combine(m, col, w, k):
+        at = pl.ds(col, w)
+        half = (A_HALF, F_HALF)[m]
+        half_rows(m, col, w, k).wait()
+        both = stacked((ma, mf)[m][rows_kept(c, m), at] + (ra, rf)[m][:, at])
+        (ta, tf)[m][:, at] = both
+        acc[:, lanes_of[m]] += dot(stacked((swa, swf)[m][:, at]), both, NT)
 
     def joined(it, first, count):
         return jnp.concatenate(
@@ -157,7 +190,7 @@
     def a_left(first, col, w):
         terms = stacked(joined(0, first, w // LANES))
         at = pl.ds(col, w)
-        acc[:, :A_PAD] += dot(terms, ma[0, :, at], NT) + dot(terms, ma[1, :, at], NT)
+        acc[:, lanes_of[0]] += dot(terms, ta[:, at], NT)
 
     def a_left_step(k, _):
         a_left(k * (A_STEP // LANES), pl.multiple_of(k * A_STEP, A_STEP), A_STEP)
@@ -166,42 +199,26 @@
     def f_left_step(k, _):
         terms = stacked(joined(0, F_FIRST + k * (F_STEP // LANES), F_STEP // LANES))
         at = pl.ds(pl.multiple_of(k * F_STEP, F_STEP), F_STEP)
-        acc[:, A_PAD:] += dot(terms, mf[0, :, at], NT) + dot(terms, mf[1, :, at], NT)
+        acc[:, lanes_of[1]] += dot(terms, tf[:, at], NT)
         return 0
 
-    mine = pl.ds(pl.multiple_of(c * HALF, HALF), HALF)
-    other = pl.ds(pl.multiple_of((1 - c) * HALF, HALF), HALF)
-    rows_of = (slice(0, A_PAD), slice(A_PAD, ROWS))
-    part, from_mate, along_z, whole = (a_part, f_part), (a_mate, f_mate), (a_z, f_z), (a_sum, f_sum)
-
-    def halves(it, m):
-        return remote(part[m].at[it, other], from_mate[m].at[it], p_send.at[it, m, 0], p_recv.at[it, m, 0], mate)
-
-    def start_halves(it, m):
-        part[m][it] = folded(acc[:, rows_of[m]])
-        halves(it, m).start()
+    along_z = (a_z, f_z)
 
     def start_z(it, m):
-        halves(it, m).wait()
-        along_z[m][it, z] = part[m][it, mine] + from_mate[m][it]
+        half = (A_HALF, F_HALF)[m]
+        product = folded(acc[:, lanes_of[m]])
+        along_z[m][it, z] = product[:, :half] + product[:, half:]
         for i in (2, 1, 3):
             at = along_z[m].at[it, z]
-            remote(at, at, p_send.at[it, m, 1], p_recv.at[it, m, 1], (along[i], s)).start()
-
-    def start_back(it, m):
+            remote(at, at, p_send.at[it, m], p_recv.at[it, m], (along[i], s)).start()
+
+    def finish_left(it, m, inverses):
         three = along_z[m].at[it, pl.ds(0, 3)]
-        remote(three, three, p_send.at[it, m, 1], p_recv.at[it, m, 1], mate).wait()
+        remote(three, three, p_send.at[it, m], p_recv.at[it, m], mate).wait()
         terms = along_z[m]
-        whole[m][it, mine] = (terms[it, 0] + terms[it, 1]) + (terms[it, 2] + terms[it, 3])
-        at = whole[m].at[it, mine]
-        remote(at, at, p_send.at[it, m, 2], p_recv.at[it, m, 2], mate).start()
-
-    def finish_left(it, m, inverses):
-        at = whole[m].at[it, other]
-        remote(at, at, p_send.at[it, m, 2], p_recv.at[it, m, 2], mate).wait()
-        left = whole[m][it]
+        left = (terms[it, 0] + terms[it, 1]) + (terms[it, 2] + terms[it, 3])
         if it == 1:
-            left = exact(inverses[m], left, NN) * (1.0 / REPLICAS)
+            left = applied(inverses[m], left) * (1.0 / REPLICAS)
         return left
 
     def keep(it, first, product):
@@ -210,9 +227,7 @@
             zl[it, 1, first + i] = product[HALF:, i * LANES : (i + 1) * LANES]
 
     def right(it, m, terms, first, col, w):
-        matrix = (ma, mf)[m]
-        at = pl.ds(col, w)
-        keep(it, first, folded(dot(terms, matrix[0, :, at], NN)) + folded(dot(terms, matrix[1, :, at], NN)))
+        keep(it, first, folded(dot(terms, (ta, tf)[m][:, pl.ds(col, w)], NN)))
 
     def right_steps(it, m, terms, begin, end):
         def step(k, _):
@@ -247,9 +262,19 @@
 
     eye = (lax.broadcasted_iota(jnp.int32, (R, R), 0) == lax.broadcasted_iota(jnp.int32, (R, R), 1)).astype(f32)
 
+    part8, other8 = pl.ds(pl.multiple_of(c * 8, 8), 8), pl.ds(pl.multiple_of((1 - c) * 8, 8), 8)
+
+    def gram_to_mate(it):
+        return remote(gt.at[it, other8], gm.at[it], h_send.at[it, 0], h_recv.at[it, 0], mate)
+
     def start_gram(it, la, lf):
-        ga, gf = exact(la, la, NT), exact(lf, lf, NT)
-        gs[it, s] = jnp.concatenate([ga[:HALF], ga[HALF:], gf[:HALF], gf[HALF:]], axis=1)
+        ga, gf = gram_of(la), gram_of(lf)
+        gt[it] = jnp.concatenate([ga[:HALF], ga[HALF:], gf[:HALF], gf[HALF:]], axis=1)
+        gram_to_mate(it).start()
+
+    def spread_gram(it):
+        gram_to_mate(it).wait()
+        gs[it, s] = gt[it, part8] + gm[it]
 
         def send(k, _):
             at = gs.at[it, s]
@@ -264,6 +289,14 @@
         gram = gs[it, 0]
         for o in range(1, PLANE):
             gram = gram + gs[it, o]
+        gz[it, part8] = gram
+        at = gz.at[it, part8]
+        copy = remote(at, at, h_send.at[it, 1], h_recv.at[it, 1], mate)
+        copy.start()
+        copy.wait_send()
+        at = gz.at[it, other8]
+        remote(at, at, h_send.at[it, 1], h_recv.at[it, 1], mate).wait_recv()
+        gram = gz[it]
         ga = jnp.concatenate([gram[:, :R], gram[:, R : 2 * R]], axis=0)
         gf = jnp.concatenate([gram[:, 2 * R : 3 * R], gram[:, 3 * R :]], axis=0)
         return inverse_factors(jnp.concatenate([ga, eye, gf, eye], axis=1))
@@ -344,14 +377,29 @@
     for it in range(2):
         if it == 0:
             load_aw.wait()
-            lax.fori_loop(0, A_FULL, a_absorb, 0)
-            absorb(sa, swa, ma, A_FULL * A_STEP, A_TAIL, A_ROWS, A_PAD, 0, A_FULL)
             pl.semaphore_wait(barrier, CHIPS)
-            start_halves(it, 0)
+            absorb(sa, 0, A_ROWS, 0, A_LOAD, 0)
+
+            def a_first(k, _):
+                absorb(sa, 0, A_ROWS, pl.multiple_of(k * A_LOAD, A_LOAD), A_LOAD, k)
+                combine(0, pl.multiple_of((k - 1) * A_LOAD, A_LOAD), A_LOAD, k - 1)
+                return 0
+
+            lax.fori_loop(1, A_LOADS, a_first, 0)
+            absorb(sa, 0, A_ROWS, A_LOADS * A_LOAD, A_REST, A_LOADS)
+            combine(0, (A_LOADS - 1) * A_LOAD, A_LOAD, A_LOADS - 1)
             load_fw.wait()
-            lax.fori_loop(0, 4, f_absorb, 0)
+            absorb(sf, 1, F_ROWS, 0, F_LOAD, A_LOADS + 1)
+            combine(0, A_LOADS * A_LOAD, A_REST, A_LOADS)
             start_z(it, 0)
-            lax.fori_loop(4, F_FULL, f_absorb, 0)
+
+            def f_first(k, _):
+                absorb(sf, 1, F_ROWS, pl.multiple_of(k * F_LOAD, F_LOAD), F_LOAD, A_LOADS + 1 + k)
+                combine(1, pl.multiple_of((k - 1) * F_LOAD, F_LOAD), F_LOAD, A_LOADS + k)
+                return 0
+
+            lax.fori_loop(1, F_LOADS, f_first, 0)
+            combine(1, (F_LOADS - 1) * F_LOAD, F_LOAD, A_LOADS + F_LOADS)
         else:
             acc[...] = jnp.zeros_like(acc)
             hand_on(0, 0)
@@ -362,20 +410,14 @@
             handed(0, 1).wait()
             lax.fori_loop(4, A_FULL, a_left_step, 0)
             a_left(A_FULL * (A_STEP // LANES), A_FULL * A_STEP, A_TAIL)
-            start_halves(it, 0)
+            start_z(it, 0)
             handed(0, 2).wait()
-            lax.fori_loop(0, 4, f_left_step, 0)
-            start_z(it, 0)
-            lax.fori_loop(4, F_FULL, f_left_step, 0)
-        start_halves(it, 1)
-        if it == 0:
-            start_back(it, 0)
-            start_z(it, 1)
-        else:
-            start_z(it, 1)
-            start_back(it, 0)
+            lax.fori_loop(0, F_COLS // F_STEP, f_left_step, 0)
+        start_z(it, 1)
+        if it == 1:
+            sent(0)
         la = finish_left(it, 0, inverses)
-        terms = stacked(la)
+        terms = twice(la)
         right_steps(it, 0, terms, 0, 4)
         to_mate(it, 0).start()
         right_steps(it, 0, terms, 4, A_FULL)
@@ -383,25 +425,32 @@
         to_mate(it, 1).start()
         if it == 0:
             scatter(it, 0)
-            start_back(it, 1)
-        else:
-            start_back(it, 1)
+            scatter(it, 1)
+        lf = finish_left(it, 1, inverses)
+        right_steps(it, 1, twice(lf), 0, F_COLS // A_STEP)
+        to_mate(it, 2).start()
+        if it == 1:
             scatter(it, 0)
-        lf = finish_left(it, 1, inverses)
-        terms = stacked(lf)
-        right_steps(it, 1, terms, 0, F_COLS // A_STEP)
-        to_mate(it, 2).start()
-        scatter(it, 1)
+            scatter(it, 1)
         scatter(it, 2)
         start_gram(it, la, lf)
+        spread_gram(it)
         gather(it)
         inverses = finish_gram(it)
         if it == 1:
-            bt[...] = jnp.concatenate([exact(inverses[0], la, NN), exact(inverses[1], lf, NN)], axis=1)
-        sent(it)
+            ba, bf = applied(inverses[0], la), applied(inverses[1], lf)
+            b_part[0] = jnp.concatenate([ba, bf], axis=1)
+            remote(b_part.at[0], b_part.at[1], b_send.at[0], b_recv.at[0], mate).start()
+
+    def place_basis():
+        remote(b_part.at[0], b_part.at[1], b_send.at[0], b_recv.at[0], mate).wait()
+        for source, core in ((0, c), (1, 1 - c)):
+            bt[:, pl.ds(pl.multiple_of(core * A_HALF, A_HALF), A_HALF)] = b_part[source, :, :A_HALF]
+            bt[:, pl.ds(pl.multiple_of(A_PAD + core * F_HALF, A_HALF), F_HALF)] = b_part[source, :, A_HALF:]
 
     wa, wf = wide(inverses[0]), wide(inverses[1])
     hand_on(1, 0)
+    place_basis()
     hand_on(1, 1)
     handed(1, 0).wait()
     a_out(wa, 0, 4)
@@ -411,6 +460,7 @@
     qa[:, A_FULL * A_STEP :] = normal(wa, joined(1, A_FULL * 4, A_TAIL // LANES))
     handed(1, 2).wait()
     f_out(wf)
+    sent(1)
 
 
 def carries(ma, mf, bt, qa, qf, ca, cf, oa, of, sa, sf, sem, q_sem):
@@ -428,8 +478,7 @@
             at = slice(col, min(col + step, cols))
             qh, ql = split(q[:, at])
             low = dot(basis[:, base : base + pad], jnp.concatenate([qh, ql, qh, ql], axis=0), TN)
-            full = m[0, :, at].astype(f32) + m[1, :, at].astype(f32) - low
-            stage[:, at] = full[:rows]
+            stage[:, at] = m[:rows, at] - low[:rows]
             copy = pltpu.make_async_copy(stage.at[:, at], out.at[0, :, at], sem.at[n])
             copy.start()
             copies.append(copy)
@@ -446,8 +495,8 @@
         sweeps,
         name="sweeps",
         out_shape=(
-            pltpu.VMEM((2, A_PAD, A_COLS), bf16),
-            pltpu.VMEM((2, F_PAD, F_COLS), bf16),
+            pltpu.VMEM((A_PAD, A_COLS), f32),
+            pltpu.VMEM((F_PAD, F_COLS), f32),
             pltpu.VMEM((R, ROWS), f32),
             pltpu.VMEM((R, A_COLS), f32),
             pltpu.VMEM((R, F_COLS), f32),
@@ -459,27 +508,35 @@
             pltpu.VMEM((2, F_ROWS, F_COLS), f32),
             pltpu.VMEM((R, A_COLS), f32),
             pltpu.VMEM((R, F_COLS), f32),
-            dma((A_FULL + 1 + F_FULL,)),
+            dma((A_LOADS + 1 + F_LOADS,)),
             dma((2,)),
+            pltpu.VMEM((A_HALF, A_COLS), f32),
+            pltpu.VMEM((F_HALF, F_COLS), f32),
+            pltpu.VMEM((A_PAD, A_COLS), bf16),
+            pltpu.VMEM((F_PAD, F_COLS), bf16),
+            dma((A_LOADS + 1 + F_LOADS,)),
+            dma((A_LOADS + 1 + F_LOADS,)),
             pltpu.VMEM((2 * R, ROWS), f32),
-            pltpu.VMEM((2, R, A_PAD), f32),
-            pltpu.VMEM((2, R, F_PAD), f32),
-            pltpu.VMEM((2, HALF, A_PAD), f32),
-            pltpu.VMEM((2, HALF, F_PAD), f32),
-            pltpu.VMEM((2, 4, HALF, A_PAD), f32),
-            pltpu.VMEM((2, 4, HALF, F_PAD), f32),
-            pltpu.VMEM((2, R, A_PAD), f32),
-            pltpu.VMEM((2, R, F_PAD), f32),
-            pltpu.VMEM((2, PLANE, HALF, LANES), f32),
+            pltpu.VMEM((2, 4, R, A_HALF), f32),
+            pltpu.VMEM((2, 4, R, F_HALF), f32),
+            pltpu.VMEM((2, R, A_HALF + F_HALF), f32),
+            pltpu.VMEM((2, PLANE, 8, LANES), f32),
+            pltpu.VMEM((2, HALF, LANES), f32),
+            pltpu.VMEM((2, 8, LANES), f32),
+            pltpu.VMEM((2, HALF, LANES), f32),
             pltpu.VMEM((2, 2, UNITS, HALF, LANES), f32),
             pltpu.VMEM((2, UNITS, HALF, LANES), f32),
             pltpu.VMEM((2, UNITS, HALF, LANES), f32),
             pltpu.VMEM((2, CHIPS, HALF, LANES), f32),
             pltpu.VMEM((2, 2, UNITS, HALF, LANES), f32),
-            dma((2, 2, 3)),
-            dma((2, 2, 3)),
+            dma((2, 2)),
+            dma((2, 2)),
+            dma((1,)),
+            dma((1,)),
             dma((2,)),
             dma((2,)),
+            dma((2, 2)),
+            dma((2, 2)),
             dma((2, 3)),
             dma((2, 3)),
             dma((2,)),

time: 79.6 us -> 76.9 us (0.966)
  Pallas kernels: 78.8 us -> 76.2 us
    pallas_call x1, Pallas kernels: 75 us -> 72.3 us  [kernel_one(): pl.pallas_call(sweeps, name='sweeps', out_shape=(pltpu.VMEM((A_PAD, A_COL...]
where the time goes in v2:
time: 76.9 us; the launch traced here: 76.8 us
  Pallas kernels  76.2 us (99%)
    pallas_call x1, Pallas kernels, kernel_one(): pl.pallas_call(sweeps, name='sweeps', out_shape=(pltpu.VMEM((A_PAD, A_COL...  72.3 us
    pallas_call x1, Pallas kernels, shards(): pl.pallas_call(carries, name='carries', out_shape=(jax.ShapeDtypeStruct((...  3.84 us

profile of v2, /device:TPU:1, one launch (start us, length us, event | category | flops | bytes accessed | tf_op | source)
XLA Modules:
  0.0 76.8 jit_solution(17583492626573650739)
XLA Ops:
  0.6 72.3 %sweeps.1 = (f32[256,3968]{1,0:T(8,128)S(1)}, f32[512,2048]{1,0:T(8,128)S(1)}, f32[32,768]{1,0:T(8,128)S(1)}, f32[32,3968]{1,0:T(8,128)S(1)}, f32[32,2048]{1,0:T(8,128)S(1)}) custom-call(f32[1,248,3968]{2,1,0:T(8,128)} %ag.1, f32[1,248,3968]{2,1,0:T(8,128)} %ae.1, f32[1,496,2048]{2,1,0:T(8,128)} %fg.1, f32[1,496,2048]{2,1,0:T(8,128)} %fe.1, f32[32,3968]{1,0:T(8,128)} %aw.1, ...), custom_call_target="tpu_custom_call" | custom-call | tf_op jit(solution)/shard_map/sweeps/pallas_call | solution.py:494
  73.0 3.8 %carries.1 = (f32[1,248,3968]{2,1,0:T(8,128)}, f32[1,496,2048]{2,1,0:T(8,128)}, f32[32,3968]{1,0:T(8,128)}, f32[32,2048]{1,0:T(8,128)}) custom-call(f32[256,3968]{1,0:T(8,128)S(1)} %get-tuple-element.9.ma, f32[512,2048]{1,0:T(8,128)S(1)} %get-tuple-element.10.mf, f32[32,768]{1,0:T(8,128)S(1)} %get-tuple-element.11.bt, f32[32,3968]{1,0:T(8,128)S(1)} %get-tuple-element.12.qa, ...), custom_call_target="tpu_custom_call" | custom-call | tf_op jit(solution)/shard_map/carries/pallas_call | solution.py:560

commit v3 on v2

--- a/solution.py
+++ b/solution.py
@@ -95,6 +95,7 @@
     ma, mf, bt, qa, qf,
     sa, sf, swa, swf, load_sem, warm_sem,
     ra, rf, ta, tf, t_send, t_recv,
+    pa, pf, na, nf, l_send, l_recv,
     acc, a_z, f_z, b_part,
     gs, gt, gm, gz, zl, zp, zs, rr, zg,
     p_send, p_recv, b_send, b_recv, g_send, g_recv, h_send, h_recv, m_send, m_recv,
@@ -159,28 +160,48 @@
     ma[A_ROWS:] = jnp.zeros((A_PAD - A_ROWS, A_COLS), f32)
     mf[F_ROWS:] = jnp.zeros((F_PAD - F_ROWS, F_COLS), f32)
 
-    def rows_kept(core, m):
+    def absorb(m, col, w, k):
+        stage, rows, pad = ((sa, A_ROWS, A_PAD), (sf, F_ROWS, F_PAD))[m]
+        at = pl.ds(col, w)
+        pltpu.make_async_copy(stage.at[:, :, at], stage.at[:, :, at], load_sem.at[k]).wait()
+        value = stage[0, :, at] + stage[1, :, at]
+        (ma, mf)[m][:rows, at] = value
+        hi, lo = split(jnp.concatenate([value, jnp.zeros((pad - rows, w), f32)], axis=0))
+        terms = stacked((swa, swf)[m][:, at])
+        acc[:, lanes_of[m]] += dot(terms, hi, NT) + dot(terms, lo, NT)
+
+    def a_absorb(k, _):
+        absorb(0, pl.multiple_of(k * A_LOAD, A_LOAD), A_LOAD, k)
+        return 0
+
+    def f_absorb(k, _):
+        absorb(1, pl.multiple_of(k * F_LOAD, F_LOAD), F_LOAD, A_LOADS + 1 + k)
+        return 0
+
+    def kept(core, m):
         half = (A_HALF, F_HALF)[m]
         return pl.ds(pl.multiple_of(core * half, half), half)
 
-    def half_rows(m, col, w, k):
-        at = pl.ds(col, w)
-        source = (ma, mf)[m].at[rows_kept(1 - c, m), at]
-        return remote(source, (ra, rf)[m].at[:, at], t_send.at[k], t_recv.at[k], mate)
-
-    def absorb(stage, m, rows, col, w, k):
-        at = pl.ds(col, w)
-        pltpu.make_async_copy(stage.at[:, :, at], stage.at[:, :, at], load_sem.at[k]).wait()
-        (ma, mf)[m][:rows, at] = stage[0, :, at] + stage[1, :, at]
-        half_rows(m, col, w, k).start()
-
-    def combine(m, col, w, k):
-        at = pl.ds(col, w)
-        half = (A_HALF, F_HALF)[m]
-        half_rows(m, col, w, k).wait()
-        both = stacked((ma, mf)[m][rows_kept(c, m), at] + (ra, rf)[m][:, at])
-        (ta, tf)[m][:, at] = both
-        acc[:, lanes_of[m]] += dot(stacked((swa, swf)[m][:, at]), both, NT)
+    def half_rows(m):
+        return remote((ma, mf)[m].at[kept(1 - c, m)], (ra, rf)[m], t_send.at[m], t_recv.at[m], mate)
+
+    def combine(m):
+        half, w, target = ((A_HALF, LANES, ta), (F_HALF, LANES, tf))[m]
+        half_rows(m).wait()
+
+        def step(k, _):
+            at = pl.ds(pl.multiple_of(k * w, w), w)
+            target[:, at] = stacked((ma, mf)[m][kept(c, m), at] + (ra, rf)[m][:, at])
+            return 0
+
+        lax.fori_loop(0, (A_COLS, F_COLS)[m] // w, step, 0)
+
+    def half_left(m):
+        return remote((pa, pf)[m].at[:, kept(1 - c, m)], (na, nf)[m], l_send.at[m], l_recv.at[m], mate)
+
+    def start_left(m):
+        (pa, pf)[m][...] = folded(acc[:, lanes_of[m]])
+        half_left(m).start()
 
     def joined(it, first, count):
         return jnp.concatenate(
@@ -206,8 +227,12 @@
 
     def start_z(it, m):
         half = (A_HALF, F_HALF)[m]
-        product = folded(acc[:, lanes_of[m]])
-        along_z[m][it, z] = product[:, :half] + product[:, half:]
+        if it == 0:
+            half_left(m).wait()
+            along_z[m][it, z] = (pa, pf)[m][:, kept(c, m)] + (na, nf)[m][...]
+        else:
+            product = folded(acc[:, lanes_of[m]])
+            along_z[m][it, z] = product[:, :half] + product[:, half:]
         for i in (2, 1, 3):
             at = along_z[m].at[it, z]
             remote(at, at, p_send.at[it, m], p_recv.at[it, m], (along[i], s)).start()
@@ -377,29 +402,16 @@
     for it in range(2):
         if it == 0:
             load_aw.wait()
+            lax.fori_loop(0, A_LOADS, a_absorb, 0)
+            absorb(0, A_LOADS * A_LOAD, A_REST, A_LOADS)
+            load_fw.wait()
+            lax.fori_loop(0, F_LOADS // 2, f_absorb, 0)
             pl.semaphore_wait(barrier, CHIPS)
-            absorb(sa, 0, A_ROWS, 0, A_LOAD, 0)
-
-            def a_first(k, _):
-                absorb(sa, 0, A_ROWS, pl.multiple_of(k * A_LOAD, A_LOAD), A_LOAD, k)
-                combine(0, pl.multiple_of((k - 1) * A_LOAD, A_LOAD), A_LOAD, k - 1)
-                return 0
-
-            lax.fori_loop(1, A_LOADS, a_first, 0)
-            absorb(sa, 0, A_ROWS, A_LOADS * A_LOAD, A_REST, A_LOADS)
-            combine(0, (A_LOADS - 1) * A_LOAD, A_LOAD, A_LOADS - 1)
-            load_fw.wait()
-            absorb(sf, 1, F_ROWS, 0, F_LOAD, A_LOADS + 1)
-            combine(0, A_LOADS * A_LOAD, A_REST, A_LOADS)
+            start_left(0)
+            half_rows(0).start()
+            lax.fori_loop(F_LOADS // 2, F_LOADS, f_absorb, 0)
+            start_left(1)
             start_z(it, 0)
-
-            def f_first(k, _):
-                absorb(sf, 1, F_ROWS, pl.multiple_of(k * F_LOAD, F_LOAD), F_LOAD, A_LOADS + 1 + k)
-                combine(1, pl.multiple_of((k - 1) * F_LOAD, F_LOAD), F_LOAD, A_LOADS + k)
-                return 0
-
-            lax.fori_loop(1, F_LOADS, f_first, 0)
-            combine(1, (F_LOADS - 1) * F_LOAD, F_LOAD, A_LOADS + F_LOADS)
         else:
             acc[...] = jnp.zeros_like(acc)
             hand_on(0, 0)
@@ -414,7 +426,10 @@
             handed(0, 2).wait()
             lax.fori_loop(0, F_COLS // F_STEP, f_left_step, 0)
         start_z(it, 1)
-        if it == 1:
+        if it == 0:
+            half_rows(1).start()
+            combine(0)
+        else:
             sent(0)
         la = finish_left(it, 0, inverses)
         terms = twice(la)
@@ -426,6 +441,8 @@
         if it == 0:
             scatter(it, 0)
             scatter(it, 1)
+        if it == 0:
+            combine(1)
         lf = finish_left(it, 1, inverses)
         right_steps(it, 1, twice(lf), 0, F_COLS // A_STEP)
         to_mate(it, 2).start()
@@ -514,8 +531,14 @@
             pltpu.VMEM((F_HALF, F_COLS), f32),
             pltpu.VMEM((A_PAD, A_COLS), bf16),
             pltpu.VMEM((F_PAD, F_COLS), bf16),
-            dma((A_LOADS + 1 + F_LOADS,)),
-            dma((A_LOADS + 1 + F_LOADS,)),
+            dma((2,)),
+            dma((2,)),
+            pltpu.VMEM((R, A_PAD), f32),
+            pltpu.VMEM((R, F_PAD), f32),
+            pltpu.VMEM((R, A_HALF), f32),
+            pltpu.VMEM((R, F_HALF), f32),
+            dma((2,)),
+            dma((2,)),
             pltpu.VMEM((2 * R, ROWS), f32),
             pltpu.VMEM((2, 4, R, A_HALF), f32),
             pltpu.VMEM((2, 4, R, F_HALF), f32),

time: 76.9 us -> 77.3 us (level)
  no operation moved by 1% of the time
where the time goes in v3:
time: 77.3 us; the launch traced here: 77.2 us
  Pallas kernels  76.6 us (99%)
    pallas_call x1, Pallas kernels, kernel_one(): pl.pallas_call(sweeps, name='sweeps', out_shape=(pltpu.VMEM((A_PAD, A_COL...  72.7 us
    pallas_call x1, Pallas kernels, shards(): pl.pallas_call(carries, name='carries', out_shape=(jax.ShapeDtypeStruct((...  3.84 us

profile of v3, /device:TPU:1, one launch (start us, length us, event | category | flops | bytes accessed | tf_op | source)
XLA Modules:
  0.0 77.2 jit_solution(15561659437903412845)
XLA Ops:
  0.6 72.7 %sweeps.1 = (f32[256,3968]{1,0:T(8,128)S(1)}, f32[512,2048]{1,0:T(8,128)S(1)}, f32[32,768]{1,0:T(8,128)S(1)}, f32[32,3968]{1,0:T(8,128)S(1)}, f32[32,2048]{1,0:T(8,128)S(1)}) custom-call(f32[1,248,3968]{2,1,0:T(8,128)} %ag.1, f32[1,248,3968]{2,1,0:T(8,128)} %ae.1, f32[1,496,2048]{2,1,0:T(8,128)} %fg.1, f32[1,496,2048]{2,1,0:T(8,128)} %fe.1, f32[32,3968]{1,0:T(8,128)} %aw.1, ...), custom_call_target="tpu_custom_call" | custom-call | tf_op jit(solution)/shard_map/sweeps/pallas_call | solution.py:511
  73.4 3.8 %carries.1 = (f32[1,248,3968]{2,1,0:T(8,128)}, f32[1,496,2048]{2,1,0:T(8,128)}, f32[32,3968]{1,0:T(8,128)}, f32[32,2048]{1,0:T(8,128)}) custom-call(f32[256,3968]{1,0:T(8,128)S(1)} %get-tuple-element.9.ma, f32[512,2048]{1,0:T(8,128)S(1)} %get-tuple-element.10.mf, f32[32,768]{1,0:T(8,128)S(1)} %get-tuple-element.11.bt, f32[32,3968]{1,0:T(8,128)S(1)} %get-tuple-element.12.qa, ...), custom_call_target="tpu_custom_call" | custom-call | tf_op jit(solution)/shard_map/carries/pallas_call | solution.py:583
